TPU v7x, 32 devices: a whole 2x2x4 slice. The times are simulated.
32 devices in a mesh: gx: 4 (over z), gy: 2 (over y), gz: 4 (over x, core).
Axes of the slice: x: 2, y: 2, z: 4, core: 2. Of those that a mesh axis runs over, the one named last changes fastest.
Arguments:
- adjoint_fields: float32 [6, 1, 16, 16, 512], P(None, None, 'gx', 'gy', 'gz'), may hold values from -6 to 6
- forward_fields: bfloat16 [2, 3, 1, 16, 16, 512], P(None, None, None, 'gx', 'gy', 'gz'), may hold values from -6 to 6
- rock_unit: int32 [16, 16, 512], P('gx', 'gy', 'gz'), may hold values from 0 to 31
- unit_conductivity: int32 [32], replicated, may hold values from 50 to 2000
- receiver_cells: int32 [256], replicated, may hold values from 0 to 131071
- residuals: float32 [2, 1, 256], replicated, may hold values from -6 to 6
- model_vectors: float32 [16, 4, 16, 512], P('gx', None, 'gy', 'gz'), may hold values from -6 to 6
Outputs:
- adjoint_state: float32 [6, 1, 16, 16, 512], P(None, None, 'gx', 'gy', 'gz')
- normal_product: float32 [16, 4, 16, 512], P('gx', None, 'gy', 'gz')
Inputs may be any that keep to these rules, and one draw needn't show every extreme that they name: `rock_unit`: each entry is a rock unit number. `receiver_cells`: a receiver's linear cell index; two receivers may share a cell.
All inputs are finite; a program needn't handle non-finite values.
Results may differ from a plain program's by a relative error of at most 0.00075.
Values sent between devices are 32-bit elements; how exact they have to be, the bound alone decides.
A program may use at most 64 MiB of HBM per device.

v0:
```python
import math

import jax
import jax.numpy as jnp
from jax import lax
from jax.sharding import PartitionSpec as P

LOSS_FACTOR = 0.5
COURANT = 0.5


def padded_2(block, sides, width):
    for axis, dim in sides:
        count = lax.axis_size(axis)
        forward = [(i, i + 1) for i in range(count - 1)]
        backward = [(target, source) for source, target in forward]
        low = lax.ppermute(
            lax.slice_in_dim(block, block.shape[dim] - width, None, axis=dim), axis, forward
        )
        high = lax.ppermute(lax.slice_in_dim(block, 0, width, axis=dim), axis, backward)
        block = jnp.concatenate([low, block, high], axis=dim)
    return block


def crop(array, outer, inner):
    cut = outer - inner
    if cut == 0:
        return array
    return array[..., cut:-cut, cut:-cut, cut:-cut]


def local(
    adjoint_fields,
    forward_fields,
    rock_unit,
    unit_conductivity,
    receiver_cells,
    residuals,
    model_vectors,
):
    moments = forward_fields.shape[0]
    sources = adjoint_fields.shape[1]
    tile_x, tile_y, tile_z = rock_unit.shape
    whole_x = tile_x * lax.axis_size("gx")
    whole_y = tile_y * lax.axis_size("gy")
    whole_z = tile_z * lax.axis_size("gz")
    unit_count = unit_conductivity.shape[0]
    labels = lax.broadcasted_iota(jnp.int32, (unit_count, 1, 1, 1), 0)
    looked_up = jnp.sum(
        jnp.where(rock_unit[None] == labels, unit_conductivity[:, None, None, None], 0), axis=0
    )
    conductivity = looked_up.astype(jnp.float32) * 0.001
    depth = 1
    damping = LOSS_FACTOR * conductivity
    keep_ext = (1.0 - damping) / (1.0 + damping)
    drive_ext = COURANT / (1.0 + damping)
    sigma_tile = crop(conductivity, depth - 1, 0)
    anchor_x = lax.axis_index("gx") * tile_x
    anchor_y = lax.axis_index("gy") * tile_y
    anchor_z = lax.axis_index("gz") * tile_z
    coord_x = lax.broadcasted_iota(jnp.int32, (tile_x + 2 * depth, 1, 1), 0) + anchor_x - depth
    coord_y = lax.broadcasted_iota(jnp.int32, (1, tile_y + 2 * depth, 1), 1) + anchor_y - depth
    coord_z = lax.broadcasted_iota(jnp.int32, (1, 1, tile_z + 2 * depth), 2) + anchor_z - depth
    inside = (
        (coord_x >= 0)
        & (coord_x < whole_x)
        & (coord_y >= 0)
        & (coord_y < whole_y)
        & (coord_z >= 0)
        & (coord_z < whole_z)
    )
    margin = depth - 1
    ext_x = tile_x + 2 * margin
    ext_y = tile_y + 2 * margin
    ext_z = tile_z + 2 * margin
    local_x = receiver_cells // (whole_y * whole_z) - anchor_x + margin
    local_y = receiver_cells // whole_z % whole_y - anchor_y + margin
    local_z = receiver_cells % whole_z - anchor_z + margin
    within = (
        (local_x >= 0)
        & (local_x < ext_x)
        & (local_y >= 0)
        & (local_y < ext_y)
        & (local_z >= 0)
        & (local_z < ext_z)
    )
    ext_cells = ext_x * ext_y * ext_z
    flat_index = jnp.where(within, (local_x * ext_y + local_y) * ext_z + local_z, ext_cells)
    state = adjoint_fields
    panels = []
    for block in range(moments // depth):
        padded = padded_2(state, (("gx", 2), ("gy", 3), ("gz", 4)), 1)
        moment = block * depth
        electric = padded[0:3]
        magnetic = padded[3:6]
        tile_e = crop(electric, depth, 0)
        forward_f = forward_fields[moment].astype(jnp.float32)
        panels.append(
            sigma_tile
            * (forward_f[0] * tile_e[0] + forward_f[1] * tile_e[1] + forward_f[2] * tile_e[2])
        )
        electric_base = electric[:, :, :-1, :-1, :-1]
        magnetic_base = magnetic[:, :, :-1, :-1, :-1]
        along_x = electric[:, :, 1:, :-1, :-1] - electric_base
        along_y = electric[:, :, :-1, 1:, :-1] - electric_base
        along_z = electric[:, :, :-1, :-1, 1:] - electric_base
        new_h = jnp.stack(
            [
                magnetic_base[0] - COURANT * (along_y[2] - along_z[1]),
                magnetic_base[1] - COURANT * (along_z[0] - along_x[2]),
                magnetic_base[2] - COURANT * (along_x[1] - along_y[0]),
            ]
        )
        h_mask = crop(inside, depth, depth)[:-1, :-1, :-1]
        new_h = jnp.where(h_mask, new_h, 0.0)
        inner_h = new_h[:, :, 1:, 1:, 1:]
        back_x = inner_h - new_h[:, :, :-1, 1:, 1:]
        back_y = inner_h - new_h[:, :, 1:, :-1, 1:]
        back_z = inner_h - new_h[:, :, 1:, 1:, :-1]
        inject_ext = (
            jnp.zeros((sources, ext_cells), jnp.float32)
            .at[:, flat_index]
            .add(residuals[moment], mode="drop")
        )
        inject_ext = inject_ext.reshape(sources, ext_x, ext_y, ext_z)
        inject = crop(inject_ext, margin, depth - 1)
        keep_rate = crop(keep_ext, margin, depth - 1)
        drive_rate = crop(drive_ext, margin, depth - 1)
        middle_e = electric[:, :, 1:-1, 1:-1, 1:-1]
        new_e = jnp.stack(
            [
                keep_rate * middle_e[0] + drive_rate * (back_y[2] - back_z[1] + inject),
                keep_rate * middle_e[1] + drive_rate * (back_z[0] - back_x[2]),
                keep_rate * middle_e[2] + drive_rate * (back_x[1] - back_y[0]),
            ]
        )
        new_e = jnp.where(crop(inside, depth, depth - 1), new_e, 0.0)
        padded = jnp.concatenate([new_e, inner_h], axis=0)
        state = padded
    panel_rows = jnp.stack(panels).reshape(moments * sources, tile_x, tile_y, tile_z)
    scale_factor = 1.0 / math.sqrt(float(moments * sources) * float(whole_x * whole_y * whole_z))
    local_w = jnp.einsum(
        "kxyz,xnyz->kn", panel_rows, model_vectors, precision=lax.Precision.HIGHEST
    )
    weights = lax.psum(local_w, ("gx", "gy", "gz"))
    normal_product = scale_factor * jnp.einsum(
        "kxyz,kn->xnyz", panel_rows, weights, precision=lax.Precision.HIGHEST
    )
    return (state, normal_product)


def solution(mesh):
    in_specs = (
        P(None, None, "gx", "gy", "gz"),
        P(None, None, None, "gx", "gy", "gz"),
        P("gx", "gy", "gz"),
        P(),
        P(),
        P(),
        P("gx", None, "gy", "gz"),
    )
    out_specs = (P(None, None, "gx", "gy", "gz"), P("gx", None, "gy", "gz"))
    return jax.shard_map(local, mesh=mesh, in_specs=in_specs, out_specs=out_specs, check_vma=False)
```

profile of v0, /device:TPU:0, one launch (start us, length us, event | category | flops | bytes accessed | tf_op | source)
XLA Modules:
  0.0 104.1 jit_solution(2446326424200641260)
XLA Ops:
  0.6 0.0 copy-start
  0.6 0.0 copy-start.2
  0.7 0.8 fusion.61
  1.5 4.9 %collective-permute-start = (f32[6,1,1,8,128]{4,3,2,1,0:T(8,128)S(1)}, f32[6,1,1,8,128]{4,3,2,1,0:T(8,128)S(1)}, u32[]{:S(2)}, u32[]{:S(2)}) collective-permute-start(f32[6,1,1,8,128]{4,3,2,1,0:T(8,128)S(1)} %get-tuple-element.45), channel_id=1, source_target_pairs={{0,8},{8,16},{16,24},{1,9},{9,17},{17,25},{2,10},{10,18},{18,26},{... | collective-permute-start | bytes 73736 | tf_op jit(solution)/shard_map/ppermute | solution.py:17
  6.4 1.3 %collective-permute-start.1 = (f32[6,1,1,8,128]{4,3,2,1,0:T(8,128)S(1)}, f32[6,1,1,8,128]{4,3,2,1,0:T(8,128)S(1)}, u32[]{:S(2)}, u32[]{:S(2)}) collective-permute-start(f32[6,1,1,8,128]{4,3,2,1,0:T(8,128)S(1)} %get-tuple-element.44), channel_id=1, source_target_pairs={{8,0},{16,8},{24,16},{9,1},{17,9},{25,17},{10,2},{18,10},{26,18},{... | collective-permute-start | bytes 73736 | tf_op jit(solution)/shard_map/ppermute | solution.py:20
  7.7 0.0 copy-done.2
  7.7 0.0 copy-start.1
  7.8 0.1 and_and_fusion.1
  7.9 0.0 copy-start.4
  7.9 0.1 and_and_fusion
  7.9 0.6 copy-done.4
  8.5 0.0 collective-permute-done
  8.5 0.1 copy-done.1
  8.7 3.4 %collective-permute-done.1 = f32[6,1,1,8,128]{4,3,2,1,0:T(8,128)S(1)} collective-permute-done((f32[6,1,1,8,128]{4,3,2,1,0:T(8,128)S(1)}, f32[6,1,1,8,128]{4,3,2,1,0:T(8,128)S(1)}, u32[]{:S(2)}, u32[]{:S(2)}) %collective-permute-start.1) | collective-permute-done | bytes 24608 | tf_op jit(solution)/shard_map/ppermute | solution.py:20
  12.1 0.0 copy-start.5
  12.1 3.4 %collective-permute-start.2 = (f32[6,1,6,1,128]{4,3,2,1,0:T(1,128)S(1)}, f32[6,1,6,1,128]{4,3,2,1,0:T(1,128)S(1)}, u32[]{:S(2)}, u32[]{:S(2)}) collective-permute-start(f32[6,1,6,1,128]{4,3,2,1,0:T(1,128)S(1)} %get-tuple-element.36), channel_id=1, source_target_pairs={{0,4},{1,5},{2,6},{3,7},{8,12},{9,13},{10,14},{11,15},{16,20},{17,... | collective-permute-start | bytes 55304 | tf_op jit(solution)/shard_map/ppermute | solution.py:17
  15.6 1.3 %collective-permute-start.3 = (f32[6,1,6,1,128]{4,3,2,1,0:T(1,128)S(1)}, f32[6,1,6,1,128]{4,3,2,1,0:T(1,128)S(1)}, u32[]{:S(2)}, u32[]{:S(2)}) collective-permute-start(f32[6,1,6,1,128]{4,3,2,1,0:T(1,128)S(1)} %get-tuple-element.37), channel_id=1, source_target_pairs={{4,0},{5,1},{6,2},{7,3},{12,8},{13,9},{14,10},{15,11},{20,16},{21,... | collective-permute-start | bytes 55304 | tf_op jit(solution)/shard_map/ppermute | solution.py:20
  16.9 0.0 copy-done.5
  16.9 0.1 collective-permute-done.2
  17.0 4.2 %collective-permute-done.3 = f32[6,1,6,1,128]{4,3,2,1,0:T(1,128)S(1)} collective-permute-done((f32[6,1,6,1,128]{4,3,2,1,0:T(1,128)S(1)}, f32[6,1,6,1,128]{4,3,2,1,0:T(1,128)S(1)}, u32[]{:S(2)}, u32[]{:S(2)}) %collective-permute-start.3) | collective-permute-done | bytes 18464 | tf_op jit(solution)/shard_map/ppermute | solution.py:20
  21.2 0.1 pad_maximum_fusion
  21.3 0.0 copy-start.3
  21.3 0.1 fusion.59
  21.5 0.0 copy-start.6
  21.5 1.3 %collective-permute-start.4 = (f32[6,1,6,10,1]{4,3,2,1,0:T(8,128)S(1)}, f32[6,1,6,10,1]{4,3,2,1,0:T(8,128)S(1)}, u32[]{:S(2)}, u32[]{:S(2)}) collective-permute-start(f32[6,1,6,10,1]{4,3,2,1,0:T(8,128)S(1)} %get-tuple-element.22), channel_id=1, source_target_pairs={{0,1},{1,2},{2,3},{4,5},{5,6},{6,7},{8,9},{9,10},{10,11},{12,13},{... | collective-permute-start | bytes 4328 | tf_op jit(solution)/shard_map/ppermute | solution.py:17
  22.8 0.0 copy-done.3
  22.8 0.0 copy-done.6
  22.8 0.1 select_reduce_fusion
  22.9 0.1 slice.401
  23.0 1.9 %scatter_custom_fusion = f32[4096]{0:T(1024)S(1)} fusion(s32[256]{0:T(256)S(1)} %compare_select_fusion, f32[256]{0:T(256)S(1)} %bitcast.93, f32[]{:T(128)} %constant.92.clone.1), kind=kCustom, calls=%fused_computation.122 | custom fusion | flops 256 | bytes 16388 | tf_op jit(solution)/shard_map/scatter-add | solution.py:123
  25.0 1.3 %collective-permute-start.5 = (f32[6,1,6,10,1]{4,3,2,1,0:T(8,128)S(1)}, f32[6,1,6,10,1]{4,3,2,1,0:T(8,128)S(1)}, u32[]{:S(2)}, u32[]{:S(2)}) collective-permute-start(f32[6,1,6,10,1]{4,3,2,1,0:T(8,128)S(1)} %get-tuple-element.21), channel_id=1, source_target_pairs={{1,0},{2,1},{3,2},{5,4},{6,5},{7,6},{9,8},{10,9},{11,10},{13,12},{... | collective-permute-start | bytes 4328 | tf_op jit(solution)/shard_map/ppermute | solution.py:20
  26.3 0.0 collective-permute-done.4
  26.3 0.4 maximum_maximum_fusion
  26.6 3.5 %collective-permute-done.5 = f32[6,1,6,10,1]{4,3,2,1,0:T(8,128)S(1)} collective-permute-done((f32[6,1,6,10,1]{4,3,2,1,0:T(8,128)S(1)}, f32[6,1,6,10,1]{4,3,2,1,0:T(8,128)S(1)}, u32[]{:S(2)}, u32[]{:S(2)}) %collective-permute-start.5) | collective-permute-done | bytes 1472 | tf_op jit(solution)/shard_map/ppermute | solution.py:20
  30.1 0.1 fusion.2
  30.2 0.2 fusion.14
  30.5 0.1 slice_subtract_fusion.14
  30.7 3.5 %collective-permute-start.6 = (f32[6,1,1,8,128]{4,3,2,1,0:T(8,128)S(1)}, f32[6,1,1,8,128]{4,3,2,1,0:T(8,128)S(1)}, u32[]{:S(2)}, u32[]{:S(2)}) collective-permute-start(f32[6,1,1,8,128]{4,3,2,1,0:T(8,128)S(1)} %get-tuple-element.42), channel_id=1, source_target_pairs={{0,8},{8,16},{16,24},{1,9},{9,17},{17,25},{2,10},{10,18},{18,26},{... | collective-permute-start | bytes 73736 | tf_op jit(solution)/shard_map/ppermute | solution.py:17
  34.2 1.3 %collective-permute-start.7 = (f32[6,1,1,8,128]{4,3,2,1,0:T(8,128)S(1)}, f32[6,1,1,8,128]{4,3,2,1,0:T(8,128)S(1)}, u32[]{:S(2)}, u32[]{:S(2)}) collective-permute-start(f32[6,1,1,8,128]{4,3,2,1,0:T(8,128)S(1)} %get-tuple-element.43), channel_id=1, source_target_pairs={{8,0},{16,8},{24,16},{9,1},{17,9},{25,17},{10,2},{18,10},{26,18},{... | collective-permute-start | bytes 73736 | tf_op jit(solution)/shard_map/ppermute | solution.py:20
  35.5 0.2 collective-permute-done.6
  35.7 4.2 %collective-permute-done.7 = f32[6,1,1,8,128]{4,3,2,1,0:T(8,128)S(1)} collective-permute-done((f32[6,1,1,8,128]{4,3,2,1,0:T(8,128)S(1)}, f32[6,1,1,8,128]{4,3,2,1,0:T(8,128)S(1)}, u32[]{:S(2)}, u32[]{:S(2)}) %collective-permute-start.7) | collective-permute-done | bytes 24608 | tf_op jit(solution)/shard_map/ppermute | solution.py:20
  39.9 1.6 %collective-permute-start.8 = (f32[6,1,6,1,128]{4,3,2,1,0:T(1,128)S(1)}, f32[6,1,6,1,128]{4,3,2,1,0:T(1,128)S(1)}, u32[]{:S(2)}, u32[]{:S(2)}) collective-permute-start(f32[6,1,6,1,128]{4,3,2,1,0:T(1,128)S(1)} %get-tuple-element.34), channel_id=1, source_target_pairs={{0,4},{1,5},{2,6},{3,7},{8,12},{9,13},{10,14},{11,15},{16,20},{17,... | collective-permute-start | bytes 55304 | tf_op jit(solution)/shard_map/ppermute | solution.py:17
  41.6 1.3 %collective-permute-start.9 = (f32[6,1,6,1,128]{4,3,2,1,0:T(1,128)S(1)}, f32[6,1,6,1,128]{4,3,2,1,0:T(1,128)S(1)}, u32[]{:S(2)}, u32[]{:S(2)}) collective-permute-start(f32[6,1,6,1,128]{4,3,2,1,0:T(1,128)S(1)} %get-tuple-element.35), channel_id=1, source_target_pairs={{4,0},{5,1},{6,2},{7,3},{12,8},{13,9},{14,10},{15,11},{20,16},{21,... | collective-permute-start | bytes 55304 | tf_op jit(solution)/shard_map/ppermute | solution.py:20
  42.9 0.1 collective-permute-done.8
  43.0 4.2 %collective-permute-done.9 = f32[6,1,6,1,128]{4,3,2,1,0:T(1,128)S(1)} collective-permute-done((f32[6,1,6,1,128]{4,3,2,1,0:T(1,128)S(1)}, f32[6,1,6,1,128]{4,3,2,1,0:T(1,128)S(1)}, u32[]{:S(2)}, u32[]{:S(2)}) %collective-permute-start.9) | collective-permute-done | bytes 18464 | tf_op jit(solution)/shard_map/ppermute | solution.py:20
  47.2 0.1 pad_maximum_fusion.1
  47.3 0.1 fusion.58
  47.4 4.1 %collective-permute-start.10 = (f32[6,1,6,10,1]{4,3,2,1,0:T(8,128)S(1)}, f32[6,1,6,10,1]{4,3,2,1,0:T(8,128)S(1)}, u32[]{:S(2)}, u32[]{:S(2)}) collective-permute-start(f32[6,1,6,10,1]{4,3,2,1,0:T(8,128)S(1)} %get-tuple-element.20), channel_id=1, source_target_pairs={{0,1},{1,2},{2,3},{4,5},{5,6},{6,7},{8,9},{9,10},{10,11},{12,13},{... | collective-permute-start | bytes 4328 | tf_op jit(solution)/shard_map/ppermute | solution.py:17
  51.6 1.9 %scatter_custom_fusion.1 = f32[4096]{0:T(1024)S(1)} fusion(s32[256]{0:T(256)S(1)} %compare_select_fusion, f32[256]{0:T(256)S(1)} %bitcast.92, f32[]{:T(128)} %constant.92.clone.1), kind=kCustom, calls=%fused_computation.120 | custom fusion | flops 256 | bytes 16388 | tf_op jit(solution)/shard_map/scatter-add | solution.py:123
  53.5 1.3 %collective-permute-start.11 = (f32[6,1,6,10,1]{4,3,2,1,0:T(8,128)S(1)}, f32[6,1,6,10,1]{4,3,2,1,0:T(8,128)S(1)}, u32[]{:S(2)}, u32[]{:S(2)}) collective-permute-start(f32[6,1,6,10,1]{4,3,2,1,0:T(8,128)S(1)} %get-tuple-element.19), channel_id=1, source_target_pairs={{1,0},{2,1},{3,2},{5,4},{6,5},{7,6},{9,8},{10,9},{11,10},{13,12},{... | collective-permute-start | bytes 4328 | tf_op jit(solution)/shard_map/ppermute | solution.py:20
  54.8 0.0 collective-permute-done.10
  54.8 0.4 maximum_maximum_fusion.1
  55.2 4.0 %collective-permute-done.11 = f32[6,1,6,10,1]{4,3,2,1,0:T(8,128)S(1)} collective-permute-done((f32[6,1,6,10,1]{4,3,2,1,0:T(8,128)S(1)}, f32[6,1,6,10,1]{4,3,2,1,0:T(8,128)S(1)}, u32[]{:S(2)}, u32[]{:S(2)}) %collective-permute-start.11) | collective-permute-done | bytes 1472 | tf_op jit(solution)/shard_map/ppermute | solution.py:20
  59.2 0.1 fusion.1
  59.3 0.1 fusion.6
  59.4 0.2 fusion.8
  59.6 0.1 slice_subtract_fusion.11
  59.8 0.0 copy-done
  59.8 0.4 convolution_bitcast_fusion
  60.1 42.4 %psum.7 = f32[2,4]{1,0:T(2,128)S(1)} all-reduce(f32[2,4]{1,0:T(2,128)S(1)} %convolution_bitcast_fusion), channel_id=1, replica_groups=mesh['gx'=4,'gy'=2,'gz'=4] {'gx','gy','gz'}, use_global_device_ids=true, to_apply=%region_3.4 | all-reduce | flops 8 | bytes 64 | tf_op jit(solution)/shard_map/psum | solution.py:145
  102.5 0.3 fusion
  102.8 0.6 copy.56
  103.5 0.6 pad_maximum_fusion.11
  (20 shorter events, 0.3 us)
Async XLA Ops:
  0.6 59.1 %copy-start = (f32[4,4,8,128]{3,2,1,0:T(8,128)S(1)}, f32[4,4,8,128]{3,2,1,0:T(8,128)}, u32[]{:S(2)}) copy-start(f32[4,4,8,128]{3,2,1,0:T(8,128)} %param.13) | copy-start | bytes 196612
  0.6 7.1 %copy-start.2 = (bf16[2,3,1,4,8,128]{5,4,3,2,1,0:T(8,128)(2,1)S(1)}, bf16[2,3,1,4,8,128]{5,4,3,2,1,0:T(8,128)(2,1)}, u32[]{:S(2)}) copy-start(bf16[2,3,1,4,8,128]{5,4,3,2,1,0:T(8,128)(2,1)} %param.8) | copy-start | bytes 147460
  1.5 7.1 %collective-permute-start = (f32[6,1,1,8,128]{4,3,2,1,0:T(8,128)S(1)}, f32[6,1,1,8,128]{4,3,2,1,0:T(8,128)S(1)}, u32[]{:S(2)}, u32[]{:S(2)}) collective-permute-start(f32[6,1,1,8,128]{4,3,2,1,0:T(8,128)S(1)} %get-tuple-element.45), channel_id=1, source_target_pairs={{0,8},{8,16},{16,24},{1,9},{9,17},{17,25},{2,10},{10,18},{18,26},{... | collective-permute-start | bytes 73736 | tf_op jit(solution)/shard_map/ppermute | solution.py:17
  6.4 5.7 %collective-permute-start.1 = (f32[6,1,1,8,128]{4,3,2,1,0:T(8,128)S(1)}, f32[6,1,1,8,128]{4,3,2,1,0:T(8,128)S(1)}, u32[]{:S(2)}, u32[]{:S(2)}) collective-permute-start(f32[6,1,1,8,128]{4,3,2,1,0:T(8,128)S(1)} %get-tuple-element.44), channel_id=1, source_target_pairs={{8,0},{16,8},{24,16},{9,1},{17,9},{25,17},{10,2},{18,10},{26,18},{... | collective-permute-start | bytes 73736 | tf_op jit(solution)/shard_map/ppermute | solution.py:20
  7.7 0.9 copy-start.1
  7.9 0.7 copy-start.4
  12.1 4.7 %copy-start.5 = (s32[256]{0:T(256)S(1)}, s32[256]{0:T(256)}, u32[]{:S(2)}) copy-start(s32[256]{0:T(256)} %param.11) | copy-start | bytes 3076
  12.1 4.9 %collective-permute-start.2 = (f32[6,1,6,1,128]{4,3,2,1,0:T(1,128)S(1)}, f32[6,1,6,1,128]{4,3,2,1,0:T(1,128)S(1)}, u32[]{:S(2)}, u32[]{:S(2)}) collective-permute-start(f32[6,1,6,1,128]{4,3,2,1,0:T(1,128)S(1)} %get-tuple-element.36), channel_id=1, source_target_pairs={{0,4},{1,5},{2,6},{3,7},{8,12},{9,13},{10,14},{11,15},{16,20},{17,... | collective-permute-start | bytes 55304 | tf_op jit(solution)/shard_map/ppermute | solution.py:17
  15.6 5.7 %collective-permute-start.3 = (f32[6,1,6,1,128]{4,3,2,1,0:T(1,128)S(1)}, f32[6,1,6,1,128]{4,3,2,1,0:T(1,128)S(1)}, u32[]{:S(2)}, u32[]{:S(2)}) collective-permute-start(f32[6,1,6,1,128]{4,3,2,1,0:T(1,128)S(1)} %get-tuple-element.37), channel_id=1, source_target_pairs={{4,0},{5,1},{6,2},{7,3},{12,8},{13,9},{14,10},{15,11},{20,16},{21,... | collective-permute-start | bytes 55304 | tf_op jit(solution)/shard_map/ppermute | solution.py:20
  21.3 1.5 %copy-start.3 = (s32[4,8,128]{2,1,0:T(8,128)S(1)}, s32[4,8,128]{2,1,0:T(8,128)}, u32[]{:S(2)}) copy-start(s32[4,8,128]{2,1,0:T(8,128)} %param.9) | copy-start | bytes 49156
  21.5 1.3 %copy-start.6 = (s32[32]{0:T(128)S(1)}, s32[32]{0:T(128)}, u32[]{:S(2)}) copy-start(s32[32]{0:T(128)} %param.10) | copy-start | bytes 388
  21.5 4.8 %collective-permute-start.4 = (f32[6,1,6,10,1]{4,3,2,1,0:T(8,128)S(1)}, f32[6,1,6,10,1]{4,3,2,1,0:T(8,128)S(1)}, u32[]{:S(2)}, u32[]{:S(2)}) collective-permute-start(f32[6,1,6,10,1]{4,3,2,1,0:T(8,128)S(1)} %get-tuple-element.22), channel_id=1, source_target_pairs={{0,1},{1,2},{2,3},{4,5},{5,6},{6,7},{8,9},{9,10},{10,11},{12,13},{... | collective-permute-start | bytes 4328 | tf_op jit(solution)/shard_map/ppermute | solution.py:17
  25.0 5.2 %collective-permute-start.5 = (f32[6,1,6,10,1]{4,3,2,1,0:T(8,128)S(1)}, f32[6,1,6,10,1]{4,3,2,1,0:T(8,128)S(1)}, u32[]{:S(2)}, u32[]{:S(2)}) collective-permute-start(f32[6,1,6,10,1]{4,3,2,1,0:T(8,128)S(1)} %get-tuple-element.21), channel_id=1, source_target_pairs={{1,0},{2,1},{3,2},{5,4},{6,5},{7,6},{9,8},{10,9},{11,10},{13,12},{... | collective-permute-start | bytes 4328 | tf_op jit(solution)/shard_map/ppermute | solution.py:20
  30.7 5.0 %collective-permute-start.6 = (f32[6,1,1,8,128]{4,3,2,1,0:T(8,128)S(1)}, f32[6,1,1,8,128]{4,3,2,1,0:T(8,128)S(1)}, u32[]{:S(2)}, u32[]{:S(2)}) collective-permute-start(f32[6,1,1,8,128]{4,3,2,1,0:T(8,128)S(1)} %get-tuple-element.42), channel_id=1, source_target_pairs={{0,8},{8,16},{16,24},{1,9},{9,17},{17,25},{2,10},{10,18},{18,26},{... | collective-permute-start | bytes 73736 | tf_op jit(solution)/shard_map/ppermute | solution.py:17
  34.2 5.7 %collective-permute-start.7 = (f32[6,1,1,8,128]{4,3,2,1,0:T(8,128)S(1)}, f32[6,1,1,8,128]{4,3,2,1,0:T(8,128)S(1)}, u32[]{:S(2)}, u32[]{:S(2)}) collective-permute-start(f32[6,1,1,8,128]{4,3,2,1,0:T(8,128)S(1)} %get-tuple-element.43), channel_id=1, source_target_pairs={{8,0},{16,8},{24,16},{9,1},{17,9},{25,17},{10,2},{18,10},{26,18},{... | collective-permute-start | bytes 73736 | tf_op jit(solution)/shard_map/ppermute | solution.py:20
  39.9 3.1 %collective-permute-start.8 = (f32[6,1,6,1,128]{4,3,2,1,0:T(1,128)S(1)}, f32[6,1,6,1,128]{4,3,2,1,0:T(1,128)S(1)}, u32[]{:S(2)}, u32[]{:S(2)}) collective-permute-start(f32[6,1,6,1,128]{4,3,2,1,0:T(1,128)S(1)} %get-tuple-element.34), channel_id=1, source_target_pairs={{0,4},{1,5},{2,6},{3,7},{8,12},{9,13},{10,14},{11,15},{16,20},{17,... | collective-permute-start | bytes 55304 | tf_op jit(solution)/shard_map/ppermute | solution.py:17
  41.6 5.7 %collective-permute-start.9 = (f32[6,1,6,1,128]{4,3,2,1,0:T(1,128)S(1)}, f32[6,1,6,1,128]{4,3,2,1,0:T(1,128)S(1)}, u32[]{:S(2)}, u32[]{:S(2)}) collective-permute-start(f32[6,1,6,1,128]{4,3,2,1,0:T(1,128)S(1)} %get-tuple-element.35), channel_id=1, source_target_pairs={{4,0},{5,1},{6,2},{7,3},{12,8},{13,9},{14,10},{15,11},{20,16},{21,... | collective-permute-start | bytes 55304 | tf_op jit(solution)/shard_map/ppermute | solution.py:20
  47.4 7.4 %collective-permute-start.10 = (f32[6,1,6,10,1]{4,3,2,1,0:T(8,128)S(1)}, f32[6,1,6,10,1]{4,3,2,1,0:T(8,128)S(1)}, u32[]{:S(2)}, u32[]{:S(2)}) collective-permute-start(f32[6,1,6,10,1]{4,3,2,1,0:T(8,128)S(1)} %get-tuple-element.20), channel_id=1, source_target_pairs={{0,1},{1,2},{2,3},{4,5},{5,6},{6,7},{8,9},{9,10},{10,11},{12,13},{... | collective-permute-start | bytes 4328 | tf_op jit(solution)/shard_map/ppermute | solution.py:17
  53.5 5.7 %collective-permute-start.11 = (f32[6,1,6,10,1]{4,3,2,1,0:T(8,128)S(1)}, f32[6,1,6,10,1]{4,3,2,1,0:T(8,128)S(1)}, u32[]{:S(2)}, u32[]{:S(2)}) collective-permute-start(f32[6,1,6,10,1]{4,3,2,1,0:T(8,128)S(1)} %get-tuple-element.19), channel_id=1, source_target_pairs={{1,0},{2,1},{3,2},{5,4},{6,5},{7,6},{9,8},{10,9},{11,10},{13,12},{... | collective-permute-start | bytes 4328 | tf_op jit(solution)/shard_map/ppermute | solution.py:20
where the time goes:
time: 105 us; the launch traced here: 104 us
  blocking collectives  42.4 us (40%)
  starting transfers between devices  26.6 us (25%)
  waiting for transfers between devices  24 us (23%)
  other arithmetic  6.79 us (6%)
  local copies, waits for them, and re-layouts  2.56 us (2%)
  between operations  1.06 us (1%)
    psum x1, blocking collectives, local(): weights = lax.psum(local_w, ('gx', 'gy', 'gz'))  42.4 us
    ppermute x6, waiting for transfers between devices, padded_2(): lax.ppermute(lax.slice_in_dim(block, 0, width, axis=dim), axis, backward)  23.6 us
    ppermute x6, starting transfers between devices, padded_2(): lax.ppermute(lax.slice_in_dim(block, block.shape[dim] - width, None, axis...  18.9 us
    ppermute x6, starting transfers between devices, padded_2(): lax.ppermute(lax.slice_in_dim(block, 0, width, axis=dim), axis, backward)  7.75 us
    scatter-add x2, other arithmetic, local(): inject_ext = jnp.zeros((sources, ext_cells), jnp.float32).at[:, flat_inde...  3.88 us
  transfers between devices with their start and end apart: 12, of which 9 were waited for; matrix products, arithmetic and copies ran while one was open for 5% of the time, Pallas kernels for 0%

commit v1 on v0

v1 whole, which is shorter than its diff:
```python
import functools
import itertools
import math

import jax
import jax.numpy as jnp
from jax import lax
from jax.experimental import pallas as pl
from jax.experimental.pallas import tpu as pltpu
from jax.sharding import PartitionSpec as P

LOSS_FACTOR = 0.5
COURANT = 0.5
AXES = ("gx", "gy", "gz")
MESH = pl.DeviceIdType.MESH
ONE_STAGE_LIMIT = 64

E_LOW = ((-1, 0, 0), (0, -1, 0), (0, 0, -1))
H_HIGH = ((1, 0, 0), (0, 1, 0), (0, 0, 1))
LINES = ((1, 0, -1), (1, -1, 0), (-1, 1, 0), (0, 1, -1), (0, -1, 1), (-1, 0, 1))
TARGETS = E_LOW + H_HIGH + LINES


def reduce_stages(sizes):
    if math.prod(sizes) <= ONE_STAGE_LIMIT:
        return ((0, 1, 2),)
    return ((2,), (1,), (0,))


def stage_offsets(stage, sizes):
    ranges = [range(sizes[a]) if a in stage else range(1) for a in range(3)]
    return [o for o in itertools.product(*ranges) if any(o)]


def kernel(sizes, scale, fields, forward, rock, unit, cells, resid, model, state_out, normal_out,
           f0, fwd, rk, un, cl, rs, mv, st, fin, hp, xlow, xhigh, tx_buf, rx_buf, pan, nrm, *rest):
    stages = reduce_stages(sizes)
    stage_count = len(stages)
    msgs, gathers = rest[:stage_count], rest[stage_count:2 * stage_count]
    in_sem, out_sem, send_sem, recv_sem = rest[2 * stage_count:2 * stage_count + 4]
    sum_send, sum_recv = rest[2 * stage_count + 4:3 * stage_count + 4], rest[3 * stage_count + 4:]
    nx, ny, nz = rk.shape
    steps = fwd.shape[0]
    vectors = mv.shape[1]
    me = [lax.axis_index(a) for a in AXES]

    loads = [
        pltpu.make_async_copy(src, dst, in_sem.at[i])
        for i, (src, dst) in enumerate(
            ((fields, f0), (rock, rk), (unit, un), (forward, fwd), (model, mv), (cells, cl), (resid, rs))
        )
    ]
    for load in loads:
        load.start()

    def exists(offset):
        ok = None
        for a in range(3):
            if offset[a] == 0:
                continue
            here = (me[a] + offset[a] >= 0) & (me[a] + offset[a] < sizes[a])
            ok = here if ok is None else ok & here
        return ok

    def around(offset):
        return tuple(me[a] + offset[a] for a in range(3))

    def wrapped(offset):
        return tuple(
            me[a] if offset[a] == 0 else lax.rem(me[a] + offset[a], sizes[a]) for a in range(3)
        )

    barrier = pltpu.get_barrier_semaphore()
    expected = 0
    for stage in stages:
        for offset in stage_offsets(stage, sizes):
            pl.semaphore_signal(barrier, inc=1, device_id=wrapped(offset), device_id_type=MESH)
            expected = expected + 1
    if stage_count > 1:
        for offset in TARGETS:
            @pl.when(exists(offset))
            def _():
                pl.semaphore_signal(barrier, inc=1, device_id=around(offset), device_id_type=MESH)
            expected = expected + exists(offset).astype(jnp.int32)

    lane = lax.broadcasted_iota(jnp.int32, (ny, nz), 1)
    row = lax.broadcasted_iota(jnp.int32, (ny, nz), 0)
    zero = jnp.zeros((ny, nz), jnp.float32)
    last_x, last_y, last_z = nx - 1, ny - 1, nz - 1
    low_exists = [jnp.where(me[a] > 0, COURANT, 0.0).astype(jnp.float32) for a in range(3)]

    def up_y(f):
        return jnp.where(row == last_y, 0.0, pltpu.roll(f, last_y, 0))

    def up_z(f):
        return jnp.where(lane == last_z, 0.0, pltpu.roll(f, last_z, 1))

    def rows_of(ref, first, second, y):
        pack = zero
        for c, comp in enumerate((first, second)):
            if comp is None:
                continue
            for x in range(nx):
                pack = jnp.where(row == c * nx + x, jnp.broadcast_to(ref[comp, x, y:y + 1, :], (ny, nz)), pack)
        return pack

    def lanes_of(planes, z):
        pack = zero
        for i, plane in enumerate(planes):
            moved = pltpu.roll(plane, (i - z) % nz, 1) if (i - z) % nz else plane
            pack = jnp.where(lane == i, moved, pack)
        return pack

    def prepare(src, step):
        ex, ey, ez = ([src[c, x] for x in range(nx)] for c in range(3))
        for x in range(nx):
            ez_x = ez[x + 1] if x < last_x else zero
            ey_x = ey[x + 1] if x < last_x else zero
            hp[step, 0, x] = src[3, x] - COURANT * ((up_y(ez[x]) - ez[x]) - (up_z(ey[x]) - ey[x]))
            hp[step, 1, x] = src[4, x] - COURANT * ((up_z(ex[x]) - ex[x]) - (ez_x - ez[x]))
            hp[step, 2, x] = src[5, x] - COURANT * ((ey_x - ey[x]) - (up_y(ex[x]) - ex[x]))
        hps = hp.at[step]
        tx_buf[step, 0] = rows_of(src, 0, 2, 0)
        tx_buf[step, 1] = lanes_of(ey + ex, 0)
        tx_buf[step, 2] = rows_of(hps, 2, 0, last_y)
        tx_buf[step, 3] = lanes_of([hp[step, 0, x] for x in range(nx)] + [hp[step, 1, x] for x in range(nx)], last_z)
        tx_buf[step, 4] = jnp.where(lane == last_z, -COURANT * pltpu.roll(ex[last_x], last_z, 1), 0.0)
        tx_buf[step, 5] = jnp.where(row == last_y, COURANT * pltpu.roll(ex[last_x], last_y, 0), 0.0)
        tx_buf[step, 6] = jnp.where(
            row == last_x, -COURANT * jnp.broadcast_to(src[1, 0, last_y:last_y + 1, :], (ny, nz)), 0.0
        )
        tx_buf[step, 7] = jnp.where(
            lane == last_z, COURANT * pltpu.roll(rows_of(src, None, 1, last_y), last_z, 1), 0.0
        )
        tx_buf[step, 8] = jnp.where(row == last_y, -COURANT * pltpu.roll(lanes_of(ez, last_z), last_y, 0), 0.0)
        at = 2 * nx - 1
        tx_buf[step, 9] = jnp.where(lane == at, COURANT * pltpu.roll(ez[0], (at - last_z) % nz, 1), 0.0)

    def halo_copy(src, step, i):
        if i == 0:
            source, target = src.at[pl.ds(1, 2), 0], xlow.at[step]
        elif i == 3:
            source, target = hp.at[step, pl.ds(1, 2), last_x], xhigh.at[step]
        else:
            slot = i - 1 if i < 3 else i - 2
            source, target = tx_buf.at[step, slot], rx_buf.at[step, slot]
        return pltpu.make_async_remote_copy(
            src_ref=source, dst_ref=target, send_sem=send_sem.at[step, i], recv_sem=recv_sem.at[step, i],
            device_id=around(TARGETS[i]), device_id_type=MESH,
        )

    def send(src, step):
        for i in range(12):
            @pl.when(exists(TARGETS[i]))
            def _():
                halo_copy(src, step, i).start()

    def receive(src, step):
        for i in range(12):
            source = exists(tuple(-d for d in TARGETS[i]))

            @pl.when(source)
            def _():
                halo_copy(src, step, i).wait_recv()

            @pl.when(jnp.logical_not(source))
            def _():
                if i == 0:
                    xlow[step] = jnp.zeros(xlow.shape[1:], jnp.float32)
                elif i == 3:
                    xhigh[step] = jnp.zeros(xhigh.shape[1:], jnp.float32)
                else:
                    rx_buf[step, i - 1 if i < 3 else i - 2] = zero

    def sent(src, step):
        for i in range(12):
            @pl.when(exists(TARGETS[i]))
            def _():
                halo_copy(src, step, i).wait_send()

    def advance(src, dst, step, keep, drive, inject):
        y_high = lambda r: jnp.broadcast_to(rx_buf[step, 0, r:r + 1, :], (ny, nz))
        z_pack = rx_buf[step, 1]
        hx, hy, hz = [], [], []
        half = jnp.float32(COURANT)
        for x in range(nx):
            z_of = lambda l: jnp.where(lane == last_z, half * pltpu.roll(z_pack, last_z - l, 1), 0.0)
            y_of = lambda r: jnp.where(row == last_y, half * y_high(r), 0.0)
            hx.append(hp[step, 0, x] + z_of(x) - y_of(nx + x))
            hy.append(hp[step, 1, x] - z_of(nx + x))
            hz.append(hp[step, 2, x] + y_of(x))
        hy[last_x] = hy[last_x] + half * xlow[step, 1]
        hz[last_x] = hz[last_x] - half * xlow[step, 0]
        for x in range(nx):
            dst[3, x], dst[4, x], dst[5, x] = hx[x], hy[x], hz[x]
        hy_x = xhigh[step, 0] + low_exists[0] * src[2, 0] + rx_buf[step, 4]
        hz_x = xhigh[step, 1] - low_exists[0] * src[1, 0] + rx_buf[step, 5]
        y_sign = jnp.where(row < nx, low_exists[1], -low_exists[1])
        z_sign = jnp.where(lane < nx, low_exists[2], -low_exists[2])
        h_y = rx_buf[step, 2] + y_sign * tx_buf[step, 0] + rx_buf[step, 6] + rx_buf[step, 7]
        h_z = rx_buf[step, 3] + z_sign * tx_buf[step, 1] + rx_buf[step, 8] + rx_buf[step, 9]

        def back_y(h, r):
            return h - jnp.where(row == 0, jnp.broadcast_to(h_y[r:r + 1, :], (ny, nz)), pltpu.roll(h, 1, 0))

        def back_z(h, l):
            below = pltpu.roll(h_z, (nz - l) % nz, 1) if l else h_z
            return h - jnp.where(lane == 0, below, pltpu.roll(h, 1, 1))

        for x in range(nx):
            dst[0, x] = keep[x] * src[0, x] + drive[x] * (
                back_y(hz[x], x) - back_z(hy[x], nx + x) + inject[x]
            )
            back_x = hz[x] - (hz[x - 1] if x else hz_x)
            dst[1, x] = keep[x] * src[1, x] + drive[x] * (back_z(hx[x], x) - back_x)
            back_x = hy[x] - (hy[x - 1] if x else hy_x)
            dst[2, x] = keep[x] * src[2, x] + drive[x] * (back_x - back_y(hx[x], nx + x))

    def panel_of(src, step, sigma):
        sums = [zero] * vectors
        for x in range(nx):
            p = sigma[x] * (
                fwd[step, 0, x].astype(jnp.float32) * src[0, x]
                + fwd[step, 1, x].astype(jnp.float32) * src[1, x]
                + fwd[step, 2, x].astype(jnp.float32) * src[2, x]
            )
            pan[step, x] = p
            sums = [s + p * mv[x, n] for n, s in enumerate(sums)]
        message = jnp.zeros((1, nz), jnp.float32)
        one_row = lax.broadcasted_iota(jnp.int32, (1, nz), 1)
        for n in range(vectors):
            total = jnp.sum(jnp.sum(sums[n], axis=0, keepdims=True), axis=1, keepdims=True)
            message = jnp.where(one_row == step * vectors + n, total, message)
        return message

    loads[0].wait()
    prepare(f0, 0)
    pl.semaphore_wait(barrier, expected)
    send(f0, 0)

    for load in loads[1:]:
        load.wait()
    sigma, keep, drive = [], [], []
    for x in range(nx):
        found = jnp.zeros((ny, nz), jnp.int32)
        units = rk[x]
        for u in range(unit.shape[0]):
            found = jnp.where(units == u, un[u], found)
        s = found.astype(jnp.float32) * 0.001
        damping = LOSS_FACTOR * s
        sigma.append(s)
        keep.append((1.0 - damping) / (1.0 + damping))
        drive.append(COURANT / (1.0 + damping))

    count = cl.shape[1]
    at = lax.broadcasted_iota(jnp.int32, (nx * ny, count), 0)
    line = (me[0] * nx + at // ny) * (sizes[1] * ny) + me[1] * ny + at % ny
    start = line * (sizes[2] * nz) + me[2] * nz
    where_cells = cl[...]
    in_row = (where_cells >= start) & (where_cells < start + nz)
    spikes = jnp.concatenate([jnp.where(in_row, rs[t], 0.0) for t in range(steps)], axis=0)
    place = lax.broadcasted_iota(jnp.int32, (nz, count), 0)
    hits = jnp.where(place == lax.rem(where_cells, nz), 1.0, 0.0)
    injected = lax.dot_general(
        spikes, hits, (((1,), (1,)), ((), ())), precision=lax.Precision.HIGHEST,
        preferred_element_type=jnp.float32,
    )
    inject = [
        [injected[(t * nx + x) * ny:(t * nx + x + 1) * ny] for x in range(nx)] for t in range(steps)
    ]
    message = panel_of(f0, 0, sigma)

    source = f0
    for step in range(steps):
        target = fin if step == steps - 1 else st.at[step]
        if step > 0:
            message = message + panel_of(source, step, sigma)
            if step == steps - 1:
                msgs[0][...] = message
                for i, offset in enumerate(stage_offsets(stages[0], sizes)):
                    sum_copy(msgs[0], gathers[0], sum_send[0], sum_recv[0], i, wrapped(offset)).start()
            prepare(source, step)
            send(source, step)
        receive(source, step)
        advance(source, target, step, keep, drive, inject[step])
        source = target
    out_state = pltpu.make_async_copy(fin, state_out, out_sem.at[0])
    out_state.start()

    for s, stage in enumerate(stages):
        offsets = stage_offsets(stage, sizes)
        if s > 0:
            msgs[s][...] = message
            for i, offset in enumerate(offsets):
                sum_copy(msgs[s], gathers[s], sum_send[s], sum_recv[s], i, wrapped(offset)).start()
        for i, offset in enumerate(offsets):
            sum_copy(msgs[s], gathers[s], sum_send[s], sum_recv[s], i, wrapped(offset)).wait_recv()
        for i in range(len(offsets)):
            message = message + gathers[s][i]
    weights = [
        [
            jnp.broadcast_to(message[:, k * vectors + n:k * vectors + n + 1] * scale, (ny, nz))
            for n in range(vectors)
        ]
        for k in range(steps)
    ]
    for x in range(nx):
        for n in range(vectors):
            total = pan[0, x] * weights[0][n]
            for k in range(1, steps):
                total = total + pan[k, x] * weights[k][n]
            nrm[x, n] = total
    out_normal = pltpu.make_async_copy(nrm, normal_out, out_sem.at[1])
    out_normal.start()

    for step in range(steps):
        sent(f0 if step == 0 else st.at[step - 1], step)
    for s, stage in enumerate(stages):
        for i, offset in enumerate(stage_offsets(stage, sizes)):
            sum_copy(msgs[s], gathers[s], sum_send[s], sum_recv[s], i, wrapped(offset)).wait_send()
    out_state.wait()
    out_normal.wait()


def sum_copy(source, target, send, recv, i, device):
    return pltpu.make_async_remote_copy(
        src_ref=source, dst_ref=target.at[i], send_sem=send.at[i], recv_sem=recv.at[i],
        device_id=device, device_id_type=MESH,
    )


def local(sizes, adjoint_fields, forward_fields, rock_unit, unit_conductivity, receiver_cells, residuals, model_vectors):
    steps = forward_fields.shape[0]
    nx, ny, nz = rock_unit.shape
    units = unit_conductivity.shape[0]
    receivers = receiver_cells.shape[0]
    vectors = model_vectors.shape[1]
    assert adjoint_fields.shape[1] == 1 and 2 * nx <= ny and steps * vectors <= nz
    cell_total = nx * ny * nz * math.prod(sizes)
    scale = 1.0 / math.sqrt(float(steps) * float(cell_total))
    fields = adjoint_fields.reshape(6, nx, ny, nz)
    forward = forward_fields.reshape(steps, 3, nx, ny, nz)
    cells = receiver_cells.reshape(1, receivers)
    stages = reduce_stages(sizes)
    counts = [len(stage_offsets(stage, sizes)) for stage in stages]
    f32 = jnp.float32
    scratch = [
        pltpu.VMEM((6, nx, ny, nz), f32),
        pltpu.VMEM(forward.shape, forward.dtype),
        pltpu.VMEM((nx, ny, nz), jnp.int32),
        pltpu.SMEM((units,), jnp.int32),
        pltpu.VMEM((1, receivers), jnp.int32),
        pltpu.VMEM(residuals.shape, f32),
        pltpu.VMEM(model_vectors.shape, f32),
        pltpu.VMEM((max(steps - 1, 1), 6, nx, ny, nz), f32),
        pltpu.VMEM((6, nx, ny, nz), f32),
        pltpu.VMEM((steps, 3, nx, ny, nz), f32),
        pltpu.VMEM((steps, 2, ny, nz), f32),
        pltpu.VMEM((steps, 2, ny, nz), f32),
        pltpu.VMEM((steps, 10, ny, nz), f32),
        pltpu.VMEM((steps, 10, ny, nz), f32),
        pltpu.VMEM((steps, nx, ny, nz), f32),
        pltpu.VMEM(model_vectors.shape, f32),
        *[pltpu.VMEM((1, nz), f32) for _ in stages],
        *[pltpu.VMEM((count, 1, nz), f32) for count in counts],
        pltpu.SemaphoreType.DMA((7,)),
        pltpu.SemaphoreType.DMA((2,)),
        pltpu.SemaphoreType.DMA((steps, 12)),
        pltpu.SemaphoreType.DMA((steps, 12)),
        *[pltpu.SemaphoreType.DMA((count,)) for count in counts],
        *[pltpu.SemaphoreType.DMA((count,)) for count in counts],
    ]
    anywhere = pl.BlockSpec(memory_space=pl.ANY)
    state, normal = pl.pallas_call(
        functools.partial(kernel, sizes, scale),
        out_shape=(
            jax.ShapeDtypeStruct(fields.shape, f32),
            jax.ShapeDtypeStruct(model_vectors.shape, f32),
        ),
        in_specs=[anywhere] * 7,
        out_specs=(anywhere, anywhere),
        scratch_shapes=scratch,
        compiler_params=pltpu.CompilerParams(
            collective_id=0, has_side_effects=True, vmem_limit_bytes=16 * 2**20
        ),
    )(fields, forward, rock_unit, unit_conductivity, cells, residuals, model_vectors)
    return state.reshape(adjoint_fields.shape), normal


def solution(mesh):
    sizes = tuple(mesh.shape[a] for a in AXES)
    in_specs = (
        P(None, None, "gx", "gy", "gz"),
        P(None, None, None, "gx", "gy", "gz"),
        P("gx", "gy", "gz"),
        P(),
        P(),
        P(),
        P("gx", None, "gy", "gz"),
    )
    out_specs = (P(None, None, "gx", "gy", "gz"), P("gx", None, "gy", "gz"))
    return jax.shard_map(
        functools.partial(local, sizes), mesh=mesh, in_specs=in_specs, out_specs=out_specs, check_vma=False
    )
```

time: 105 us -> 21 us (0.20)
  blocking collectives: 42.4 us -> 0 us
  starting transfers between devices: 26.6 us -> 0 us
  waiting for transfers between devices: 24 us -> 0 us
  Pallas kernels: 0 us -> 14.8 us
  other arithmetic: 6.79 us -> 0 us
  local copies, waits for them, and re-layouts: 2.56 us -> 5.19 us
    psum x1 -> x0, blocking collectives: 42.4 us -> none  [local(): weights = lax.psum(local_w, ('gx', 'gy', 'gz'))]
    ppermute x12 -> x0, starting transfers between devices: 26.6 us -> none  [the longest x6 18.9 us: padded_2(): lax.ppermute(lax.slice_in_dim(block, block.shape[dim] - width, None, axis...]
    ppermute x12 -> x0, waiting for transfers between devices: 24 us -> none  [the longest x6 23.6 us: padded_2(): lax.ppermute(lax.slice_in_dim(block, 0, width, axis=dim), axis, backward)]
    pallas_call x0 -> x1, Pallas kernels: none -> 14.8 us  [local(): pl.pallas_call(functools.partial(kernel, sizes, scale), out_shape=(jax.Sh...]
    scatter-add x2 -> x0, other arithmetic: 3.88 us -> none  [local(): inject_ext = jnp.zeros((sources, ext_cells), jnp.float32).at[:, flat_inde...]
    unnamed x17 -> x16, local copies, waits for them, and re-layouts: 1.37 us -> 5.19 us
    concatenate x5 -> x0, other arithmetic: 1.51 us -> none  [the longest x4 0.86 us: padded_2(): block = jnp.concatenate([low, block, high], axis=dim)]
    slice x7 -> x0, local copies, waits for them, and re-layouts: 1.19 us -> none  [the longest x3 1.08 us: padded_2(): lax.slice_in_dim(block, 0, width, axis=dim)]
  transfers between devices with their start and end apart: 12 -> 0, of which waited for: 9 -> 0; matrix products, arithmetic and copies ran while one was open for 5% -> 0% of each run, Pallas kernels for 0% -> 0%
where the time goes in v1:
time: 21 us; the launch traced here: 20.7 us
  Pallas kernels  14.8 us (70%)
  local copies, waits for them, and re-layouts  5.19 us (25%)
  between operations  0.67 us (3%)
    pallas_call x1, Pallas kernels, local(): pl.pallas_call(functools.partial(kernel, sizes, scale), out_shape=(jax.Sh...  14.8 us
    unnamed x16, local copies, waits for them, and re-layouts  5.19 us

profile of v1, /device:TPU:0, one launch (start us, length us, event | category | flops | bytes accessed | tf_op | source)
XLA Modules:
  0.0 20.7 jit_solution(17943158082842275561)
XLA Ops:
  0.6 0.0 copy-start.4
  0.6 0.0 copy-start.5
  0.7 0.0 copy-start.6
  0.7 0.7 %copy-done.4 = f32[2,1,256]{2,1,0:T(1,128)S(1)} copy-done((f32[2,1,256]{2,1,0:T(1,128)S(1)}, f32[2,1,256]{2,1,0:T(1,128)}, u32[]{:S(2)}) %copy-start.4) | copy-done | bytes 2072
  1.3 0.0 copy-done.5
  1.3 0.0 copy-done.6
  1.3 0.0 copy-start
  1.3 0.9 %copy-done = f32[6,1,4,8,128]{4,3,2,1,0:T(8,128)S(1)} copy-done((f32[6,1,4,8,128]{4,3,2,1,0:T(8,128)S(1)}, f32[6,1,4,8,128]{4,3,2,1,0:T(8,128)}, u32[]{:S(2)}) %copy-start) | copy-done | bytes 98328
  2.2 0.0 copy-start.1
  2.2 0.8 %copy-done.1 = f32[4,4,8,128]{3,2,1,0:T(8,128)S(1)} copy-done((f32[4,4,8,128]{3,2,1,0:T(8,128)S(1)}, f32[4,4,8,128]{3,2,1,0:T(8,128)}, u32[]{:S(2)}) %copy-start.1) | copy-done | bytes 65560
  3.1 0.0 copy-start.2
  3.1 0.8 %copy-done.2 = bf16[2,3,1,4,8,128]{5,4,3,2,1,0:T(8,128)(2,1)S(1)} copy-done((bf16[2,3,1,4,8,128]{5,4,3,2,1,0:T(8,128)(2,1)S(1)}, bf16[2,3,1,4,8,128]{5,4,3,2,1,0:T(8,128)(2,1)}, u32[]{:S(2)}) %copy-start.2) | copy-done | bytes 49176
  3.9 0.0 copy-start.3
  3.9 0.7 %copy-done.3 = s32[4,8,128]{2,1,0:T(8,128)S(1)} copy-done((s32[4,8,128]{2,1,0:T(8,128)S(1)}, s32[4,8,128]{2,1,0:T(8,128)}, u32[]{:S(2)}) %copy-start.3) | copy-done | bytes 16408
  4.6 14.8 %shard_map.86 = (f32[6,4,8,128]{3,2,1,0:T(8,128)S(1)}, f32[4,4,8,128]{3,2,1,0:T(8,128)S(1)}) custom-call(f32[6,4,8,128]{3,2,1,0:T(8,128)S(1)} %bitcast.6, bf16[2,3,4,8,128]{4,3,2,1,0:T(8,128)(2,1)S(1)} %bitcast.8, s32[4,8,128]{2,1,0:T(8,128)S(1)} %copy-done.3, s32[32]{0:T(128)S(1)} %copy-done.6, s32[1,256]{1,0:T(1,128)S(1)} %bitcast.9, ...), custom_call_target="tpu_custom_call" | custom-call | tf_op jit(solution)/shard_map/pallas_call | solution.py:374
  19.4 0.6 %copy.12 = f32[6,1,4,8,128]{4,3,2,1,0:T(8,128)} copy(f32[6,1,4,8,128]{4,3,2,1,0:T(8,128)S(1)} %bitcast.7) | data formatting | bytes 196608
  20.0 0.6 %copy.13 = f32[4,4,8,128]{3,2,1,0:T(8,128)} copy(f32[4,4,8,128]{3,2,1,0:T(8,128)S(1)} %get-tuple-element.11) | data formatting | bytes 131072
Async XLA Ops:
  0.6 0.7 %copy-start.4 = (f32[2,1,256]{2,1,0:T(1,128)S(1)}, f32[2,1,256]{2,1,0:T(1,128)}, u32[]{:S(2)}) copy-start(f32[2,1,256]{2,1,0:T(1,128)} %resid.1) | copy-start | bytes 6148
  0.6 0.7 %copy-start.5 = (s32[256]{0:T(256)S(1)}, s32[256]{0:T(256)}, u32[]{:S(2)}) copy-start(s32[256]{0:T(256)} %param.11) | copy-start | bytes 3076
  0.7 0.7 %copy-start.6 = (s32[32]{0:T(128)S(1)}, s32[32]{0:T(128)}, u32[]{:S(2)}) copy-start(s32[32]{0:T(128)} %unit.1) | copy-start | bytes 388
  1.3 0.9 %copy-start = (f32[6,1,4,8,128]{4,3,2,1,0:T(8,128)S(1)}, f32[6,1,4,8,128]{4,3,2,1,0:T(8,128)}, u32[]{:S(2)}) copy-start(f32[6,1,4,8,128]{4,3,2,1,0:T(8,128)} %param.7) | copy-start | bytes 294916
  2.2 0.8 %copy-start.1 = (f32[4,4,8,128]{3,2,1,0:T(8,128)S(1)}, f32[4,4,8,128]{3,2,1,0:T(8,128)}, u32[]{:S(2)}) copy-start(f32[4,4,8,128]{3,2,1,0:T(8,128)} %model.1) | copy-start | bytes 196612
  3.1 0.8 %copy-start.2 = (bf16[2,3,1,4,8,128]{5,4,3,2,1,0:T(8,128)(2,1)S(1)}, bf16[2,3,1,4,8,128]{5,4,3,2,1,0:T(8,128)(2,1)}, u32[]{:S(2)}) copy-start(bf16[2,3,1,4,8,128]{5,4,3,2,1,0:T(8,128)(2,1)} %param.8) | copy-start | bytes 147460
  3.9 0.7 %copy-start.3 = (s32[4,8,128]{2,1,0:T(8,128)S(1)}, s32[4,8,128]{2,1,0:T(8,128)}, u32[]{:S(2)}) copy-start(s32[4,8,128]{2,1,0:T(8,128)} %rock.1) | copy-start | bytes 49156

commit v2 on v1

--- a/solution.py
+++ b/solution.py
@@ -32,13 +32,13 @@
     return [o for o in itertools.product(*ranges) if any(o)]
 
 
-def kernel(sizes, scale, fields, forward, rock, unit, cells, resid, model, state_out, normal_out,
-           f0, fwd, rk, un, cl, rs, mv, st, fin, hp, xlow, xhigh, tx_buf, rx_buf, pan, nrm, *rest):
+def kernel(sizes, fields, forward, rock, unit, cells, resid, model, fin, pan, weights,
+           f0, fwd, rk, un, cl, rs, mv, st, hp, xlow, xhigh, tx_buf, rx_buf, *rest):
     stages = reduce_stages(sizes)
     stage_count = len(stages)
     msgs, gathers = rest[:stage_count], rest[stage_count:2 * stage_count]
-    in_sem, out_sem, send_sem, recv_sem = rest[2 * stage_count:2 * stage_count + 4]
-    sum_send, sum_recv = rest[2 * stage_count + 4:3 * stage_count + 4], rest[3 * stage_count + 4:]
+    in_sem, send_sem, recv_sem = rest[2 * stage_count:2 * stage_count + 3]
+    sum_send, sum_recv = rest[2 * stage_count + 3:3 * stage_count + 3], rest[3 * stage_count + 3:]
     nx, ny, nz = rk.shape
     steps = fwd.shape[0]
     vectors = mv.shape[1]
@@ -284,8 +284,6 @@
         receive(source, step)
         advance(source, target, step, keep, drive, inject[step])
         source = target
-    out_state = pltpu.make_async_copy(fin, state_out, out_sem.at[0])
-    out_state.start()
 
     for s, stage in enumerate(stages):
         offsets = stage_offsets(stage, sizes)
@@ -297,27 +295,30 @@
             sum_copy(msgs[s], gathers[s], sum_send[s], sum_recv[s], i, wrapped(offset)).wait_recv()
         for i in range(len(offsets)):
             message = message + gathers[s][i]
-    weights = [
-        [
-            jnp.broadcast_to(message[:, k * vectors + n:k * vectors + n + 1] * scale, (ny, nz))
-            for n in range(vectors)
-        ]
-        for k in range(steps)
-    ]
-    for x in range(nx):
-        for n in range(vectors):
-            total = pan[0, x] * weights[0][n]
-            for k in range(1, steps):
-                total = total + pan[k, x] * weights[k][n]
-            nrm[x, n] = total
-    out_normal = pltpu.make_async_copy(nrm, normal_out, out_sem.at[1])
-    out_normal.start()
+    weights[...] = message
 
     for step in range(steps):
         sent(f0 if step == 0 else st.at[step - 1], step)
     for s, stage in enumerate(stages):
         for i, offset in enumerate(stage_offsets(stage, sizes)):
             sum_copy(msgs[s], gathers[s], sum_send[s], sum_recv[s], i, wrapped(offset)).wait_send()
+
+
+def finish(scale, state, pan, weights, state_out, normal_out, nrm, out_sem):
+    out_state = pltpu.make_async_copy(state, state_out, out_sem.at[0])
+    out_state.start()
+    steps, nx, ny, nz = pan.shape
+    vectors = nrm.shape[1]
+    message = weights[...] * scale
+    spread = [jnp.broadcast_to(message[:, i:i + 1], (ny, nz)) for i in range(steps * vectors)]
+    for x in range(nx):
+        for n in range(vectors):
+            total = pan[0, x] * spread[n]
+            for k in range(1, steps):
+                total = total + pan[k, x] * spread[k * vectors + n]
+            nrm[x, n] = total
+    out_normal = pltpu.make_async_copy(nrm, normal_out, out_sem.at[1])
+    out_normal.start()
     out_state.wait()
     out_normal.wait()
 
@@ -353,37 +354,46 @@
         pltpu.VMEM(residuals.shape, f32),
         pltpu.VMEM(model_vectors.shape, f32),
         pltpu.VMEM((max(steps - 1, 1), 6, nx, ny, nz), f32),
-        pltpu.VMEM((6, nx, ny, nz), f32),
         pltpu.VMEM((steps, 3, nx, ny, nz), f32),
         pltpu.VMEM((steps, 2, ny, nz), f32),
         pltpu.VMEM((steps, 2, ny, nz), f32),
         pltpu.VMEM((steps, 10, ny, nz), f32),
         pltpu.VMEM((steps, 10, ny, nz), f32),
-        pltpu.VMEM((steps, nx, ny, nz), f32),
-        pltpu.VMEM(model_vectors.shape, f32),
         *[pltpu.VMEM((1, nz), f32) for _ in stages],
         *[pltpu.VMEM((count, 1, nz), f32) for count in counts],
         pltpu.SemaphoreType.DMA((7,)),
-        pltpu.SemaphoreType.DMA((2,)),
         pltpu.SemaphoreType.DMA((steps, 12)),
         pltpu.SemaphoreType.DMA((steps, 12)),
         *[pltpu.SemaphoreType.DMA((count,)) for count in counts],
         *[pltpu.SemaphoreType.DMA((count,)) for count in counts],
     ]
-    anywhere = pl.BlockSpec(memory_space=pl.ANY)
+    hbm = pl.BlockSpec(memory_space=pltpu.HBM)
+    vmem = pl.BlockSpec(memory_space=pltpu.VMEM)
+    state, panel, weights = pl.pallas_call(
+        functools.partial(kernel, sizes),
+        out_shape=(
+            pltpu.VMEM(fields.shape, f32),
+            pltpu.VMEM((steps, nx, ny, nz), f32),
+            pltpu.VMEM((1, nz), f32),
+        ),
+        in_specs=[hbm] * 7,
+        out_specs=(vmem, vmem, vmem),
+        scratch_shapes=scratch,
+        compiler_params=pltpu.CompilerParams(
+            collective_id=0, has_side_effects=True, vmem_limit_bytes=60 * 2**20
+        ),
+    )(fields, forward, rock_unit, unit_conductivity, cells, residuals, model_vectors)
     state, normal = pl.pallas_call(
-        functools.partial(kernel, sizes, scale),
+        functools.partial(finish, scale),
         out_shape=(
             jax.ShapeDtypeStruct(fields.shape, f32),
             jax.ShapeDtypeStruct(model_vectors.shape, f32),
         ),
-        in_specs=[anywhere] * 7,
-        out_specs=(anywhere, anywhere),
-        scratch_shapes=scratch,
-        compiler_params=pltpu.CompilerParams(
-            collective_id=0, has_side_effects=True, vmem_limit_bytes=16 * 2**20
-        ),
-    )(fields, forward, rock_unit, unit_conductivity, cells, residuals, model_vectors)
+        in_specs=[vmem, vmem, vmem],
+        out_specs=(hbm, hbm),
+        scratch_shapes=[pltpu.VMEM(model_vectors.shape, f32), pltpu.SemaphoreType.DMA((2,))],
+        compiler_params=pltpu.CompilerParams(vmem_limit_bytes=16 * 2**20),
+    )(state, panel, weights)
     return state.reshape(adjoint_fields.shape), normal
 
 

time: 21 us -> 15.7 us (0.75)
  local copies, waits for them, and re-layouts: 5.19 us -> 0 us
    unnamed x16 -> x0, local copies, waits for them, and re-layouts: 5.19 us -> none
    pallas_call x1 -> x2, Pallas kernels: 14.8 us -> 14.9 us  [the longest x1 14.2 us: local(): pl.pallas_call(functools.partial(kernel, sizes), out_shape=(pltpu.VMEM(fi...]
where the time goes in v2:
time: 15.7 us; the launch traced here: 15.6 us
  Pallas kernels  14.9 us (95%)
  between operations  0.64 us (4%)
    pallas_call x1, Pallas kernels, local(): pl.pallas_call(functools.partial(kernel, sizes), out_shape=(pltpu.VMEM(fi...  14.2 us
    pallas_call x1, Pallas kernels, local(): pl.pallas_call(functools.partial(finish, scale), out_shape=(jax.ShapeDtyp...  0.73 us

profile of v2, /device:TPU:0, one launch (start us, length us, event | category | flops | bytes accessed | tf_op | source)
XLA Modules:
  0.0 15.6 jit_solution(728360489721538814)
XLA Ops:
  0.6 14.2 %shard_map.86 = (f32[6,4,8,128]{3,2,1,0:T(8,128)S(1)}, f32[2,4,8,128]{3,2,1,0:T(8,128)S(1)}, f32[1,128]{1,0:T(1,128)S(1)}) custom-call(f32[6,4,8,128]{3,2,1,0:T(8,128)} %bitcast.6, bf16[2,3,4,8,128]{4,3,2,1,0:T(8,128)(2,1)} %bitcast.7, s32[4,8,128]{2,1,0:T(8,128)} %rock.1, s32[32]{0:T(128)} %unit.1, s32[1,256]{1,0:T(1,128)} %bitcast.8, f32[2,1,256]{2,1,0:T(1,128)} %resid.1, ...), custom_call_target="tpu_custom_call" | custom-call | tf_op jit(solution)/shard_map/pallas_call | solution.py:372
  14.8 0.7 %shard_map.87 = (f32[6,4,8,128]{3,2,1,0:T(8,128)}, f32[4,4,8,128]{3,2,1,0:T(8,128)}) custom-call(f32[6,4,8,128]{3,2,1,0:T(8,128)S(1)} %get-tuple-element.7.state, f32[2,4,8,128]{3,2,1,0:T(8,128)S(1)} %get-tuple-element.8.pan, f32[1,128]{1,0:T(1,128)S(1)} %get-tuple-element.9.weights), custom_call_target="tpu_custom_call" | custom-call | tf_op jit(solution)/shard_map/pallas_call | solution.py:386

commit v3 on v2

--- a/solution.py
+++ b/solution.py
@@ -19,6 +19,7 @@
 H_HIGH = ((1, 0, 0), (0, 1, 0), (0, 0, 1))
 LINES = ((1, 0, -1), (1, -1, 0), (-1, 1, 0), (0, 1, -1), (0, -1, 1), (-1, 0, 1))
 TARGETS = E_LOW + H_HIGH + LINES
+E_FIRST, H_NEXT = (6, 7, 8, 9, 10, 11, 0, 1, 2), (3, 4, 5)
 
 
 def reduce_stages(sizes):
@@ -29,7 +30,7 @@
 
 def stage_offsets(stage, sizes):
     ranges = [range(sizes[a]) if a in stage else range(1) for a in range(3)]
-    return [o for o in itertools.product(*ranges) if any(o)]
+    return [o for o in itertools.product(*ranges) if any(o)][::-1]
 
 
 def kernel(sizes, fields, forward, rock, unit, cells, resid, model, fin, pan, weights,
@@ -111,19 +112,8 @@
             pack = jnp.where(lane == i, moved, pack)
         return pack
 
-    def prepare(src, step):
+    def prepare_lines(src, step):
         ex, ey, ez = ([src[c, x] for x in range(nx)] for c in range(3))
-        for x in range(nx):
-            ez_x = ez[x + 1] if x < last_x else zero
-            ey_x = ey[x + 1] if x < last_x else zero
-            hp[step, 0, x] = src[3, x] - COURANT * ((up_y(ez[x]) - ez[x]) - (up_z(ey[x]) - ey[x]))
-            hp[step, 1, x] = src[4, x] - COURANT * ((up_z(ex[x]) - ex[x]) - (ez_x - ez[x]))
-            hp[step, 2, x] = src[5, x] - COURANT * ((ey_x - ey[x]) - (up_y(ex[x]) - ex[x]))
-        hps = hp.at[step]
-        tx_buf[step, 0] = rows_of(src, 0, 2, 0)
-        tx_buf[step, 1] = lanes_of(ey + ex, 0)
-        tx_buf[step, 2] = rows_of(hps, 2, 0, last_y)
-        tx_buf[step, 3] = lanes_of([hp[step, 0, x] for x in range(nx)] + [hp[step, 1, x] for x in range(nx)], last_z)
         tx_buf[step, 4] = jnp.where(lane == last_z, -COURANT * pltpu.roll(ex[last_x], last_z, 1), 0.0)
         tx_buf[step, 5] = jnp.where(row == last_y, COURANT * pltpu.roll(ex[last_x], last_y, 0), 0.0)
         tx_buf[step, 6] = jnp.where(
@@ -135,6 +125,19 @@
         tx_buf[step, 8] = jnp.where(row == last_y, -COURANT * pltpu.roll(lanes_of(ez, last_z), last_y, 0), 0.0)
         at = 2 * nx - 1
         tx_buf[step, 9] = jnp.where(lane == at, COURANT * pltpu.roll(ez[0], (at - last_z) % nz, 1), 0.0)
+        tx_buf[step, 0] = rows_of(src, 0, 2, 0)
+        tx_buf[step, 1] = lanes_of(ey + ex, 0)
+
+    def prepare_curl(src, step):
+        ex, ey, ez = ([src[c, x] for x in range(nx)] for c in range(3))
+        for x in range(nx):
+            ez_x = ez[x + 1] if x < last_x else zero
+            ey_x = ey[x + 1] if x < last_x else zero
+            hp[step, 0, x] = src[3, x] - COURANT * ((up_y(ez[x]) - ez[x]) - (up_z(ey[x]) - ey[x]))
+            hp[step, 1, x] = src[4, x] - COURANT * ((up_z(ex[x]) - ex[x]) - (ez_x - ez[x]))
+            hp[step, 2, x] = src[5, x] - COURANT * ((ey_x - ey[x]) - (up_y(ex[x]) - ex[x]))
+        tx_buf[step, 2] = rows_of(hp.at[step], 2, 0, last_y)
+        tx_buf[step, 3] = lanes_of([hp[step, 0, x] for x in range(nx)] + [hp[step, 1, x] for x in range(nx)], last_z)
 
     def halo_copy(src, step, i):
         if i == 0:
@@ -149,8 +152,8 @@
             device_id=around(TARGETS[i]), device_id_type=MESH,
         )
 
-    def send(src, step):
-        for i in range(12):
+    def send(src, step, which):
+        for i in which:
             @pl.when(exists(TARGETS[i]))
             def _():
                 halo_copy(src, step, i).start()
@@ -234,9 +237,10 @@
         return message
 
     loads[0].wait()
-    prepare(f0, 0)
+    prepare_lines(f0, 0)
+    prepare_curl(f0, 0)
     pl.semaphore_wait(barrier, expected)
-    send(f0, 0)
+    send(f0, 0, E_FIRST + H_NEXT)
 
     for load in loads[1:]:
         load.wait()
@@ -274,13 +278,15 @@
     for step in range(steps):
         target = fin if step == steps - 1 else st.at[step]
         if step > 0:
+            prepare_lines(source, step)
+            send(source, step, E_FIRST)
             message = message + panel_of(source, step, sigma)
             if step == steps - 1:
                 msgs[0][...] = message
                 for i, offset in enumerate(stage_offsets(stages[0], sizes)):
                     sum_copy(msgs[0], gathers[0], sum_send[0], sum_recv[0], i, wrapped(offset)).start()
-            prepare(source, step)
-            send(source, step)
+            prepare_curl(source, step)
+            send(source, step, H_NEXT)
         receive(source, step)
         advance(source, target, step, keep, drive, inject[step])
         source = target

time: 15.7 us -> 15.6 us (level)
  no operation moved by 1% of the time
where the time goes in v3:
time: 15.6 us; the launch traced here: 15.4 us
  Pallas kernels  14.8 us (95%)
  between operations  0.64 us (4%)
    pallas_call x1, Pallas kernels, local(): pl.pallas_call(functools.partial(kernel, sizes), out_shape=(pltpu.VMEM(fi...  14 us
    pallas_call x1, Pallas kernels, local(): pl.pallas_call(functools.partial(finish, scale), out_shape=(jax.ShapeDtyp...  0.73 us

profile of v3, /device:TPU:0, one launch (start us, length us, event | category | flops | bytes accessed | tf_op | source)
XLA Modules:
  0.0 15.4 jit_solution(8596425805396449630)
XLA Ops:
  0.6 14.0 %shard_map.86 = (f32[6,4,8,128]{3,2,1,0:T(8,128)S(1)}, f32[2,4,8,128]{3,2,1,0:T(8,128)S(1)}, f32[1,128]{1,0:T(1,128)S(1)}) custom-call(f32[6,4,8,128]{3,2,1,0:T(8,128)} %bitcast.6, bf16[2,3,4,8,128]{4,3,2,1,0:T(8,128)(2,1)} %bitcast.7, s32[4,8,128]{2,1,0:T(8,128)} %rock.1, s32[32]{0:T(128)} %unit.1, s32[1,256]{1,0:T(1,128)} %bitcast.8, f32[2,1,256]{2,1,0:T(1,128)} %resid.1, ...), custom_call_target="tpu_custom_call" | custom-call | tf_op jit(solution)/shard_map/pallas_call | solution.py:378
  14.7 0.7 %shard_map.87 = (f32[6,4,8,128]{3,2,1,0:T(8,128)}, f32[4,4,8,128]{3,2,1,0:T(8,128)}) custom-call(f32[6,4,8,128]{3,2,1,0:T(8,128)S(1)} %get-tuple-element.7.state, f32[2,4,8,128]{3,2,1,0:T(8,128)S(1)} %get-tuple-element.8.pan, f32[1,128]{1,0:T(1,128)S(1)} %get-tuple-element.9.weights), custom_call_target="tpu_custom_call" | custom-call | tf_op jit(solution)/shard_map/pallas_call | solution.py:392
